TPU v7x, 32 devices: a whole 2x2x4 slice. The times are simulated.
32 devices in a mesh: dp: 8 (over y, x, core), fsdp: 4 (over z).
Axes of the slice: x: 2, y: 2, z: 4, core: 2. Of those that a mesh axis runs over, the one named last changes fastest.
Arguments:
- rollout_rows: bfloat16 [4096, 8192], P(('dp', 'fsdp')), may hold values from -6 to 6
- lengths: int32 [32, 8], P(('dp', 'fsdp')), may hold values from 1 to 32, as said below
- dest: int32 [32, 8], P(('dp', 'fsdp')), may hold values from 0 to 7, as said below
- offset: int32 [32, 8], P(('dp', 'fsdp')), may hold values from 0 to 96, as said below
- query: bfloat16 [4096, 4096], P(('dp', 'fsdp')), may hold values from -100 to 100
- key_rows: bfloat16 [4096, 512], P(('dp', 'fsdp')), may hold values from -5 to 5
- value_weight: bfloat16 [8192, 512], P('fsdp'), may hold values from -0.0625 to 0.0625
- d_out: bfloat16 [4096, 4096], P(('dp', 'fsdp')), may hold values from -6 to 6
Outputs:
- attn_out: bfloat16 [4096, 4096], P(('dp', 'fsdp'))
- grad_query: bfloat16 [4096, 4096], P(('dp', 'fsdp'))
- grad_key: bfloat16 [4096, 512], P(('dp', 'fsdp'))
- grad_input: bfloat16 [4096, 8192], P(('dp', 'fsdp'))
- grad_weight: float32 [8192, 512], P(('dp', 'fsdp'))
Inputs may be any that keep to these rules, and one draw needn't show every extreme that they name: Each rollout device's 8 lengths sum to 128. `dest`: the learner has the sender's fsdp index; the sequences of one device go to 8 different learner devices. `offset`: the sequences that a learner device receives cover its 128 rows exactly once; on every learner device the last of them is one of 32 rows.
All inputs are finite; a program needn't handle non-finite values.
Results may differ from a plain program's by a relative error of at most 0.006.
Values may be sent and summed in bfloat16 or wider, within the bound.
A program may use at most 128 MiB of HBM per device.

v0:
```python
import math
import jax
import jax.numpy as jnp
from jax import lax
from jax.sharding import PartitionSpec as P

HEAD_SIZE = 128
QUERY_HEADS = 32
KEY_VALUE_HEADS = 4


def attend(block_queries, block_keys, block_values, segment, gradient_block):
    row_count_total = block_queries.shape[0]
    share_ratio = QUERY_HEADS // KEY_VALUE_HEADS
    score_scale = 1.0 / math.sqrt(HEAD_SIZE)
    heads_queries = block_queries.reshape(row_count_total, KEY_VALUE_HEADS, share_ratio, HEAD_SIZE)
    heads_keys = block_keys.reshape(row_count_total, KEY_VALUE_HEADS, HEAD_SIZE)
    heads_values = block_values.reshape(row_count_total, KEY_VALUE_HEADS, HEAD_SIZE)
    gradient_heads = gradient_block.reshape(
        row_count_total, KEY_VALUE_HEADS, share_ratio, HEAD_SIZE
    )
    logit_scores = (
        jnp.einsum("euaz,nuz->uaen", heads_queries, heads_keys, preferred_element_type=jnp.float32)
        * score_scale
    )
    position = jnp.arange(row_count_total, dtype=jnp.int32)
    allowed = (segment[:, None] == segment[None, :]) & (position[None, :] <= position[:, None])
    logit_scores = jnp.where(allowed, logit_scores, -1e30)
    highest = jnp.max(logit_scores, axis=-1, keepdims=True)
    expo = jnp.exp(logit_scores - highest)
    probs = expo / jnp.sum(expo, axis=-1, keepdims=True)
    probs_reduced = probs.astype(jnp.bfloat16)
    attention_output = jnp.einsum(
        "yxmd,dya->myxa", probs_reduced, heads_values, preferred_element_type=jnp.float32
    )
    attention_output = attention_output.reshape(row_count_total, QUERY_HEADS * HEAD_SIZE).astype(
        jnp.bfloat16
    )
    gradient_probs = jnp.einsum(
        "euaz,nuz->uaen", gradient_heads, heads_values, preferred_element_type=jnp.float32
    )
    value_gradient = jnp.einsum(
        "lbjm,jlbw->mlw", probs_reduced, gradient_heads, preferred_element_type=jnp.float32
    )
    value_gradient = value_gradient.reshape(row_count_total, KEY_VALUE_HEADS * HEAD_SIZE).astype(
        jnp.bfloat16
    )
    inner = jnp.sum(probs * gradient_probs, axis=-1, keepdims=True)
    gradient_scores = (probs * (gradient_probs - inner) * score_scale).astype(jnp.bfloat16)
    query_gradient = jnp.einsum(
        "yxmd,dya->myxa", gradient_scores, heads_keys, preferred_element_type=jnp.float32
    )
    key_gradient = jnp.einsum(
        "lbjm,jlbw->mlw", gradient_scores, heads_queries, preferred_element_type=jnp.float32
    )
    return (
        attention_output,
        query_gradient.reshape(row_count_total, QUERY_HEADS * HEAD_SIZE).astype(jnp.bfloat16),
        key_gradient.reshape(row_count_total, KEY_VALUE_HEADS * HEAD_SIZE).astype(jnp.bfloat16),
        value_gradient,
    )


def tables(plan, tok_rows):
    seq_len, dest, offset = (plan[:, 0], plan[:, 1], plan[:, 2])
    order = jnp.arange(seq_len.shape[1], dtype=jnp.int32)
    earlier = order[None, :] < order[:, None]
    starts = jnp.sum(jnp.where(earlier[None], seq_len[:, None, :], 0), axis=2)
    rows = jnp.arange(tok_rows, dtype=jnp.int32)[None, :, None]
    inside = (rows >= starts[:, None, :]) & (rows < (starts + seq_len)[:, None, :])
    landing = (dest * tok_rows + offset - starts)[:, None, :] + rows
    return jnp.sum(jnp.where(inside, landing, 0), axis=2).reshape(-1)


def senders(plan, me, tok_rows):
    seq_len, dest, offset = (plan[:, 0], plan[:, 1], plan[:, 2])
    mine = dest == me
    land_off = jnp.sum(jnp.where(mine, offset, 0), axis=1)
    land_len = jnp.sum(jnp.where(mine, seq_len, 0), axis=1)
    rows = jnp.arange(tok_rows, dtype=jnp.int32)[:, None]
    inside = (rows >= land_off[None, :]) & (rows < (land_off + land_len)[None, :])
    source = jnp.arange(plan.shape[0], dtype=jnp.int32)
    return jnp.sum(jnp.where(inside, source[None, :], 0), axis=1)


def local(rollout_rows, lengths, dest, offset, query, key_rows, value_weight, d_out):
    n_dp = lax.axis_size("dp")
    n_fsdp = lax.axis_size("fsdp")
    me = lax.axis_index("dp")
    tok_rows = rollout_rows.shape[0]
    column = tok_rows * n_dp
    plan = lax.all_gather(jnp.concatenate([lengths, dest, offset], axis=0), "dp", axis=0)
    shared = lax.all_to_all(rollout_rows, "dp", split_axis=1, concat_axis=0, tiled=True)
    block = value_weight.shape[0] // n_dp
    piece = lax.dynamic_slice_in_dim(value_weight, me * block, block, axis=0)
    pairs = [(a * n_fsdp + b, b * n_dp + a) for a in range(n_dp) for b in range(n_fsdp)]
    piece = lax.ppermute(piece, ("dp", "fsdp"), pairs)
    weight = lax.all_gather(piece, "fsdp", axis=0, tiled=True)
    landing = tables(plan, tok_rows)
    pick = (jnp.arange(column, dtype=jnp.int32)[:, None] == landing[None, :]).astype(jnp.bfloat16)
    rows = jnp.dot(pick, shared, preferred_element_type=jnp.float32).astype(jnp.bfloat16)
    partial = jnp.dot(rows, weight, preferred_element_type=jnp.float32).astype(jnp.bfloat16)
    parts = lax.all_to_all(
        partial.reshape(n_dp, tok_rows, partial.shape[1]),
        "dp",
        split_axis=0,
        concat_axis=0,
        tiled=True,
    )
    values = jnp.sum(parts.astype(jnp.float32), axis=0).astype(jnp.bfloat16)
    attention_output, query_gradient, key_gradient, value_gradient = attend(
        query, key_rows, values, senders(plan, me, tok_rows), d_out
    )
    gathered = lax.all_gather(value_gradient, "dp", axis=0, tiled=True)
    grad_weight = lax.psum_scatter(
        lax.dot_general(
            rows, gathered, (((0,), (0,)), ((), ())), preferred_element_type=jnp.float32
        ),
        "fsdp",
        scatter_dimension=0,
        tiled=True,
    )
    grad_weight = grad_weight * (1.0 / math.sqrt(column * n_fsdp))
    share = lax.dot_general(
        gathered, weight, (((1,), (1,)), ((), ())), preferred_element_type=jnp.float32
    ).astype(jnp.bfloat16)
    grad_input = lax.all_to_all(share, "dp", split_axis=0, concat_axis=1, tiled=True)
    return (attention_output, query_gradient, key_gradient, grad_input, grad_weight)


def solution(mesh):
    in_specs = (
        P(("dp", "fsdp"), None),
        P(("dp", "fsdp"), None),
        P(("dp", "fsdp"), None),
        P(("dp", "fsdp"), None),
        P(("dp", "fsdp"), None),
        P(("dp", "fsdp"), None),
        P("fsdp", None),
        P(("dp", "fsdp"), None),
    )
    out_specs = (
        P(("dp", "fsdp"), None),
        P(("dp", "fsdp"), None),
        P(("dp", "fsdp"), None),
        P(("dp", "fsdp"), None),
        P(("dp", "fsdp"), None),
    )
    return jax.shard_map(local, mesh=mesh, in_specs=in_specs, out_specs=out_specs, check_vma=False)
```

profile of v0, /device:TPU:0, one launch (start us, length us, event | category | flops | bytes accessed | tf_op | source)
XLA Modules:
  0.0 167.1 jit_solution(17855206566767428514)
XLA Ops:
  7.2 0.8 add_bitcast_fusion
  8.1 10.3 %all-gather.1 = s32[8,3,8]{2,1,0:T(4,128)S(1)} all-gather(s32[1,3,8]{2,1,0:T(4,128)S(1)} %add_bitcast_fusion), channel_id=2, replica_groups=mesh['dp'=8,'fsdp'=4] {'dp'}, dimensions={0}, use_global_device_ids=true | all-gather | bytes 864 | tf_op jit(solution)/shard_map/all_gather | solution.py:92
  18.8 0.9 reshape.70
  19.9 2.3 %copy.127 = bf16[128,4096]{0,1:T(8,128)(2,1)} copy(bf16[128,4096]{1,0:T(8,128)(2,1)} %param.12) | data formatting | bytes 2097152 | tf_op jit(solution)/shard_map/reshape | solution.py:16
  22.2 1.6 copy.128
  23.8 3.4 %fusion.31 = (f32[4,8,128]{2,1,0:T(8,128)S(1)}, f32[4,8,128,128]{2,3,1,0:T(8,128)}) fusion(pred[128,128]{0,1:T(8,128)(4,1)S(1)} %fusion.19, bf16[128,4,128,1]{0,2,3,1:T(8,128)(2,1)S(1)} %copy.113, bf16[128,4,8,128]{0,3,2,1:T(8,128)(2,1)} %bitcast.113), kind=kOutput, calls=%fused_computation.59 | convolution fusion | flops 136315008 | bytes 3309568 | tf_op jit(solution)/shard_map/sub | solution.py:30
  27.2 2.7 %fusion.10 = bf16[4,128,128]{1,2,0:T(8,128)(2,1)} fusion(bf16[128,4,8,128]{0,3,2,1:T(8,128)(2,1)S(1)} %bitcast.108, f32[4,8,128,128]{2,3,1,0:T(8,128)} %get-tuple-element.38, f32[4,8,128]{2,1,0:T(8,128)S(1)} %get-tuple-element.37), kind=kOutput, calls=%fused_computation.21 | convolution fusion | flops 135331840 | bytes 3293184 | tf_op jit(solution)/shard_map/lbjm,jlbw->mlw/dot_general | solution.py:42
  30.0 4.1 %copy.90 = bf16[128,8192]{0,1:T(8,128)(2,1)} copy(bf16[128,8192]{1,0:T(8,128)(2,1)} %param.8) | data formatting | bytes 4194304 | tf_op args[0]
  34.0 4.4 %all-to-all-start = ((bf16[128,8,1024]{0,2,1:T(8,128)(2,1)}), bf16[128,8,1024]{0,2,1:T(8,128)(2,1)}, u32[]{:S(2)}, u32[]{:S(2)}) async-start(bf16[128,8,1024]{0,2,1:T(8,128)(2,1)} %bitcast.107), calls=%async_computation | async-start | bytes 4194304 | tf_op jit(solution)/shard_map/all_to_all | solution.py:93
  38.5 0.7 collective-permute-start
  39.2 0.7 copy-done.2
  40.3 30.3 %all-to-all-done = bf16[128,8,1024]{0,2,1:T(8,128)(2,1)} async-done(((bf16[128,8,1024]{0,2,1:T(8,128)(2,1)}), bf16[128,8,1024]{0,2,1:T(8,128)(2,1)}, u32[]{:S(2)}, u32[]{:S(2)}) %all-to-all-start) | async-done | bytes 2097184 | tf_op jit(solution)/shard_map/all_to_all | solution.py:93
  70.7 3.9 %copy.91 = bf16[8,128,1024]{2,1,0:T(8,128)(2,1)} copy(bf16[8,128,1024]{1,2,0:T(8,128)(2,1)} %bitcast.7) | data formatting | bytes 4194304 | tf_op jit(solution)/shard_map/all_to_all | solution.py:93
  74.6 5.3 %fusion.7 = bf16[1024,1024]{1,0:T(8,128)(2,1)} fusion(bf16[1024,1024]{1,0:T(8,128)(2,1)} %bitcast.112, s32[1024]{0:T(1024)S(1)} %bitcast.130), kind=kOutput, calls=%fused_computation.12 | convolution fusion | flops 2149580800 | bytes 4198400 | tf_op jit(solution)/shard_map/dot_general | solution.py:101
  79.8 4.5 %fusion.33 = f32[1024,512]{1,0:T(8,128)} fusion(bf16[1024,1024]{1,0:T(8,128)(2,1)} %fusion.7, bf16[1024,512]{0,1:T(8,128)(2,1)} %all-gather.7.cloned.1.call-done), kind=kOutput, calls=%fused_computation.61 | convolution fusion | flops 1073741824 | bytes 5242880 | tf_op jit(solution)/shard_map/dot_general | solution.py:116
  84.4 16.3 %all-gather.5.cloned.1.call-done = bf16[1024,512]{1,0:T(8,128)(2,1)} async-done(((bf16[256,512]{1,0:T(8,128)(2,1)}), bf16[1024,512]{1,0:T(8,128)(2,1)}) %all-gather.5.cloned.1.call-update) | async-done | bytes 1048592 | tf_op jit(solution)/shard_map/all_gather | solution.py:98
  100.7 4.1 %convolution_convert_fusion.3 = bf16[1024,512]{1,0:T(8,128)(2,1)} fusion(bf16[1024,1024]{1,0:T(8,128)(2,1)} %fusion.7, bf16[1024,512]{1,0:T(8,128)(2,1)} %all-gather.5.cloned.1.call-done), kind=kOutput, calls=%fused_computation.17 | convolution fusion | flops 1074266112 | bytes 4194304 | tf_op jit(solution)/shard_map/dot_general | solution.py:102
  104.7 4.2 %all-to-all-start.1 = ((bf16[8,128,512]{2,1,0:T(8,128)(2,1)}), bf16[8,128,512]{2,1,0:T(8,128)(2,1)}, u32[]{:S(2)}, u32[]{:S(2)}) async-start(bf16[8,128,512]{2,1,0:T(8,128)(2,1)} %bitcast.115), calls=%async_computation.1 | async-start | bytes 2097152 | tf_op jit(solution)/shard_map/all_to_all | solution.py:103
  109.0 4.2 %convolution_convert_fusion = bf16[1024,1024]{1,0:T(8,128)(2,1)} fusion(bf16[1024,512]{0,1:T(8,128)(2,1)} %all-gather.7.cloned.1.call-done, bf16[1024,512]{1,0:T(8,128)(2,1)} %all-gather.5.cloned.1.call-done), kind=kOutput, calls=%fused_computation.13 | convolution fusion | flops 1074790400 | bytes 4194304 | tf_op jit(solution)/shard_map/dot_general | solution.py:124
  113.2 11.2 %all-to-all-done.1 = bf16[8,128,512]{2,1,0:T(8,128)(2,1)} async-done(((bf16[8,128,512]{2,1,0:T(8,128)(2,1)}), bf16[8,128,512]{2,1,0:T(8,128)(2,1)}, u32[]{:S(2)}, u32[]{:S(2)}) %all-to-all-start.1) | async-done | bytes 1048608 | tf_op jit(solution)/shard_map/all_to_all | solution.py:103
  124.4 4.7 %all-to-all-start.2 = ((bf16[8,128,1024]{2,1,0:T(8,128)(2,1)}), bf16[8,128,1024]{2,1,0:T(8,128)(2,1)}, u32[]{:S(2)}, u32[]{:S(2)}) async-start(bf16[8,128,1024]{2,1,0:T(8,128)(2,1)} %bitcast.110), calls=%async_computation.2 | async-start | bytes 4194304 | tf_op jit(solution)/shard_map/all_to_all | solution.py:127
  129.1 1.4 reduce_sum.80
  130.6 3.0 %convolution_convert_fusion.2 = bf16[4,128,8,128]{3,1,2,0:T(8,128)(2,1)} fusion(bf16[128,4,128,1]{0,2,3,1:T(8,128)(2,1)S(1)} %bitcast.118, f32[4,8,128,128]{2,3,1,0:T(8,128)} %get-tuple-element.38, f32[4,8,128]{2,1,0:T(8,128)S(1)} %copy-done.4), kind=kOutput, calls=%fused_computation.16 | convolution fusion | flops 135790592 | bytes 3293184 | tf_op jit(solution)/shard_map/yxmd,dya->myxa/dot_general | solution.py:33
  133.6 2.3 %copy.105 = bf16[128,4096]{1,0:T(8,128)(2,1)} copy(bf16[128,4096]{0,1:T(8,128)(2,1)} %bitcast.117) | data formatting | bytes 2097152
  135.9 1.8 %fusion.32 = f32[4,128,128,8]{2,1,3,0:T(8,128)} fusion(bf16[128,4,128,1]{0,2,3,1:T(8,128)(2,1)S(1)} %bitcast.119, bf16[128,4,8,128]{0,3,2,1:T(8,128)(2,1)S(1)} %bitcast.109), kind=kOutput, calls=%fused_computation.60 | convolution fusion | flops 134217728 | bytes 3276800 | tf_op jit(solution)/shard_map/euaz,nuz->uaen/dot_general | solution.py:39
  137.7 5.4 %convolution_convert_fusion.1 = bf16[4,8,128,128]{2,3,1,0:T(8,128)(2,1)} fusion(bf16[128,4,128,1]{0,2,3,1:T(8,128)(2,1)S(1)} %copy.113, f32[4,128,128,8]{2,1,3,0:T(8,128)} %fusion.32, f32[4,8,128,128]{2,3,1,0:T(8,128)} %get-tuple-element.38, f32[4,8,128]{2,1,0:T(8,128)S(1)} %copy-done.4), kind=kOutput, calls=%fused_computation.15 | convolution fusion | flops 138416256 | bytes 5390336 | tf_op jit(solution)/shard_map/yxmd,dya->myxa/dot_general | solution.py:50
  143.1 2.4 %copy.106 = bf16[128,4096]{1,0:T(8,128)(2,1)} copy(bf16[128,4096]{0,1:T(8,128)(2,1)} %bitcast.116) | data formatting | bytes 2097152
  145.4 4.4 %fusion.9 = bf16[4,128,128]{1,2,0:T(8,128)(2,1)S(1)} fusion(bf16[128,4,8,128]{0,3,2,1:T(8,128)(2,1)S(1)} %bitcast.114, f32[4,128,128,8]{2,1,3,0:T(8,128)} %fusion.32, f32[4,8,128,128]{2,3,1,0:T(8,128)} %get-tuple-element.38, f32[4,8,128]{2,1,0:T(8,128)S(1)} %copy-done.4), kind=kOutput, calls=%fused_computation.20 | convolution fusion | flops 137957504 | bytes 5390336 | tf_op jit(solution)/shard_map/lbjm,jlbw->mlw/dot_general | solution.py:53
  149.8 0.8 copy.107
  150.6 5.0 %all-to-all-done.2 = bf16[8,128,1024]{2,1,0:T(8,128)(2,1)} async-done(((bf16[8,128,1024]{2,1,0:T(8,128)(2,1)}), bf16[8,128,1024]{2,1,0:T(8,128)(2,1)}, u32[]{:S(2)}, u32[]{:S(2)}) %all-to-all-start.2) | async-done | bytes 2097184 | tf_op jit(solution)/shard_map/all_to_all | solution.py:127
  155.6 3.1 %copy.129 = bf16[8,16,8,1024]{3,2,0,1:T(8,128)(2,1)} copy(bf16[8,16,8,1024]{3,2,1,0:T(8,128)(2,1)} %bitcast.49) | data formatting | bytes 4194304 | tf_op jit(solution)/shard_map/all_to_all | solution.py:127
  158.7 1.9 %broadcast_multiply_fusion = f32[256,512]{1,0:T(8,128)} fusion(f32[256,512]{1,0:T(8,128)} %reduce-scatter.2.cloned.1.call-done), kind=kLoop, calls=%fused_computation.29 | loop fusion | flops 131072 | bytes 1048576 | tf_op jit(solution)/shard_map/mul | solution.py:123
  (30 shorter events, 1.2 us)
Async XLA Ops:
  7.2 31.3 %copy-start = (bf16[2048,512]{1,0:T(8,128)(2,1)S(1)}, bf16[2048,512]{1,0:T(8,128)(2,1)}, u32[]{:S(2)}) copy-start(bf16[2048,512]{1,0:T(8,128)(2,1)} %param.14) | copy-start | bytes 6291460
  7.2 72.7 %all-gather.7.cloned.1.call-start = ((), (), s32[]{:S(2)}) async-start(), calls=%async_computation.5 | async-start | bytes 1179648 | tf_op jit(solution)/shard_map/all_gather | solution.py:114
  27.2 2.7 %copy-start.3 = (f32[4,8,128]{2,1,0:T(8,128)}, f32[4,8,128]{2,1,0:T(8,128)S(1)}, u32[]{:S(2)}) copy-start(f32[4,8,128]{2,1,0:T(8,128)S(1)} %get-tuple-element.37) | copy-start | bytes 49156
  34.0 36.6 %all-to-all-start = ((bf16[128,8,1024]{0,2,1:T(8,128)(2,1)}), bf16[128,8,1024]{0,2,1:T(8,128)(2,1)}, u32[]{:S(2)}, u32[]{:S(2)}) async-start(bf16[128,8,1024]{0,2,1:T(8,128)(2,1)} %bitcast.107), calls=%async_computation | async-start | bytes 4194304 | tf_op jit(solution)/shard_map/all_to_all | solution.py:93
  38.4 62.2 %all-gather.5.cloned.1.call-start = ((), (), s32[]{:S(2)}) async-start(), calls=%async_computation.4 | async-start | bytes 1310720 | tf_op jit(solution)/shard_map/all_gather | solution.py:98
  38.5 0.7 collective-permute-start
  39.2 0.7 copy-start.2
  39.9 118.8 %reduce-scatter.2.cloned.1.call-start = ((), (), s32[]{:S(2)}) async-start(), calls=%async_computation.6 | async-start | bytes 2621440 | tf_op jit(solution)/shard_map/reduce_scatter | solution.py:115
  104.7 19.7 %all-to-all-start.1 = ((bf16[8,128,512]{2,1,0:T(8,128)(2,1)}), bf16[8,128,512]{2,1,0:T(8,128)(2,1)}, u32[]{:S(2)}, u32[]{:S(2)}) async-start(bf16[8,128,512]{2,1,0:T(8,128)(2,1)} %bitcast.115), calls=%async_computation.1 | async-start | bytes 2097152 | tf_op jit(solution)/shard_map/all_to_all | solution.py:103
  124.4 6.2 %copy-start.4 = (f32[4,8,128]{2,1,0:T(8,128)S(1)}, f32[4,8,128]{2,1,0:T(8,128)}, u32[]{:S(2)}) copy-start(f32[4,8,128]{2,1,0:T(8,128)} %copy-done.3) | copy-start | bytes 49156
  124.4 31.2 %all-to-all-start.2 = ((bf16[8,128,1024]{2,1,0:T(8,128)(2,1)}), bf16[8,128,1024]{2,1,0:T(8,128)(2,1)}, u32[]{:S(2)}, u32[]{:S(2)}) async-start(bf16[8,128,1024]{2,1,0:T(8,128)(2,1)} %bitcast.110), calls=%async_computation.2 | async-start | bytes 4194304 | tf_op jit(solution)/shard_map/all_to_all | solution.py:127
  143.1 2.4 %copy-start.1 = (bf16[128,4096]{0,1:T(8,128)(2,1)S(1)}, bf16[128,4096]{0,1:T(8,128)(2,1)}, u32[]{:S(2)}) copy-start(bf16[128,4096]{0,1:T(8,128)(2,1)} %copy.127) | copy-start | bytes 3145732
Sparse Core Ops, SparseCore 0:
  30.1 37.2 all-gather.6
  69.5 31.0 all-gather.4
  103.0 43.3 reduce-scatter.1
where the time goes:
time: 168 us; the launch traced here: 167 us
  waiting for transfers between devices  62.9 us (37%)
  matrix products  38.7 us (23%)
  local copies, waits for them, and re-layouts  22.4 us (13%)
  starting transfers between devices  14.1 us (8%)
  between operations  13.9 us (8%)
  blocking collectives  10.3 us (6%)
  other arithmetic  4.77 us (3%)
    all_to_all x1, waiting for transfers between devices, local(): lax.all_to_all(rollout_rows, 'dp', split_axis=1, concat_axis=0, tiled=True)  30.3 us
    all_gather x1, waiting for transfers between devices, local(): weight = lax.all_gather(piece, 'fsdp', axis=0, tiled=True)  16.3 us
    all_to_all x1, waiting for transfers between devices, local(): lax.all_to_all(partial.reshape(n_dp, tok_rows, partial.shape[1]), 'dp', s...  11.2 us
    all_gather x1, blocking collectives, local(): lax.all_gather(jnp.concatenate([lengths, dest, offset], axis=0), 'dp', ax...  10.3 us
    unnamed x14, local copies, waits for them, and re-layouts  10.2 us
    dot_general x1, matrix products, attend(): jnp.einsum('yxmd,dya->myxa', gradient_scores, heads_keys, preferred_eleme...  5.38 us
    dot_general x1, matrix products, local(): jnp.dot(pick, shared, preferred_element_type=jnp.float32)  5.25 us
    all_to_all x1, waiting for transfers between devices, local(): lax.all_to_all(share, 'dp', split_axis=0, concat_axis=1, tiled=True)  5 us
  transfers between devices with their start and end apart: 7, of which 4 were waited for; matrix products, arithmetic and copies ran while one was open for 31% of the time, Pallas kernels for 0%

commit v1 on v0

--- a/solution.py
+++ b/solution.py
@@ -95,7 +95,14 @@
     piece = lax.dynamic_slice_in_dim(value_weight, me * block, block, axis=0)
     pairs = [(a * n_fsdp + b, b * n_dp + a) for a in range(n_dp) for b in range(n_fsdp)]
     piece = lax.ppermute(piece, ("dp", "fsdp"), pairs)
-    weight = lax.all_gather(piece, "fsdp", axis=0, tiled=True)
+    ways, here = (lax.axis_size("fsdp"), lax.axis_index("fsdp"))
+    weight, reach = (piece, 1)
+    while reach < ways:
+        theirs = lax.ppermute(weight, "fsdp", [(d, d ^ reach) for d in range(ways)])
+        mine_first = jnp.concatenate([weight, theirs], axis=0)
+        theirs_first = jnp.concatenate([theirs, weight], axis=0)
+        weight = jnp.where(here & reach == 0, mine_first, theirs_first)
+        reach = 2 * reach
     landing = tables(plan, tok_rows)
     pick = (jnp.arange(column, dtype=jnp.int32)[:, None] == landing[None, :]).astype(jnp.bfloat16)
     rows = jnp.dot(pick, shared, preferred_element_type=jnp.float32).astype(jnp.bfloat16)

time: 168 us -> 219 us (1.30)
  waiting for transfers between devices: 62.9 us -> 88 us
  blocking collectives: 10.3 us -> 29.6 us
  starting transfers between devices: 14.1 us -> 20.5 us
  local copies, waits for them, and re-layouts: 22.4 us -> 20 us
    ppermute x0 -> x2, waiting for transfers between devices: none -> 56.9 us  [local(): theirs = lax.ppermute(weight, 'fsdp', [(d, d ^ reach) for d in range(ways)])]
    all_to_all x1, waiting for transfers between devices: 30.3 us -> 0.01 us  [local(): lax.all_to_all(rollout_rows, 'dp', split_axis=1, concat_axis=0, tiled=True)]
    all_gather x1, blocking collectives: 10.3 us -> 29.6 us  [local(): lax.all_gather(jnp.concatenate([lengths, dest, offset], axis=0), 'dp', ax...]
    all_gather x1 -> x0, waiting for transfers between devices: 16.3 us -> none  [local(): weight = lax.all_gather(piece, 'fsdp', axis=0, tiled=True)]
    all_gather x1, waiting for transfers between devices: 0.01 us -> 15 us  [local(): gathered = lax.all_gather(value_gradient, 'dp', axis=0, tiled=True)]
    ppermute x0 -> x2, starting transfers between devices: none -> 4.8 us  [local(): theirs = lax.ppermute(weight, 'fsdp', [(d, d ^ reach) for d in range(ways)])]
    unnamed x14 -> x24, local copies, waits for them, and re-layouts: 10.2 us -> 9.65 us
  transfers between devices with their start and end apart: 7 -> 8, of which waited for: 4 -> 5; matrix products, arithmetic and copies ran while one was open for 31% -> 27% of each run, Pallas kernels for 0% -> 0%
where the time goes in v1:
time: 219 us; the launch traced here: 218 us
  waiting for transfers between devices  88 us (40%)
  matrix products  39.1 us (18%)
  blocking collectives  29.6 us (14%)
  starting transfers between devices  20.5 us (9%)
  local copies, waits for them, and re-layouts  20 us (9%)
  between operations  14.2 us (6%)
  other arithmetic  6.5 us (3%)
    ppermute x2, waiting for transfers between devices, local(): theirs = lax.ppermute(weight, 'fsdp', [(d, d ^ reach) for d in range(ways)])  56.9 us
    all_gather x1, blocking collectives, local(): lax.all_gather(jnp.concatenate([lengths, dest, offset], axis=0), 'dp', ax...  29.6 us
    all_gather x1, waiting for transfers between devices, local(): gathered = lax.all_gather(value_gradient, 'dp', axis=0, tiled=True)  15 us
    all_to_all x1, waiting for transfers between devices, local(): lax.all_to_all(partial.reshape(n_dp, tok_rows, partial.shape[1]), 'dp', s...  10.9 us
    unnamed x24, local copies, waits for them, and re-layouts  9.65 us
    dot_general x1, matrix products, attend(): jnp.einsum('yxmd,dya->myxa', gradient_scores, heads_keys, preferred_eleme...  5.36 us
    all_to_all x1, starting transfers between devices, local(): lax.all_to_all(rollout_rows, 'dp', split_axis=1, concat_axis=0, tiled=True)  5.31 us
    dot_general x1, matrix products, local(): jnp.dot(pick, shared, preferred_element_type=jnp.float32)  5.25 us
  transfers between devices with their start and end apart: 8, of which 5 were waited for; matrix products, arithmetic and copies ran while one was open for 27% of the time, Pallas kernels for 0%

profile of v1, /device:TPU:0, one launch (start us, length us, event | category | flops | bytes accessed | tf_op | source)
XLA Modules:
  0.0 218.0 jit_solution(14829762827828014881)
XLA Ops:
  7.2 4.2 %copy.90 = bf16[128,8192]{0,1:T(8,128)(2,1)} copy(bf16[128,8192]{1,0:T(8,128)(2,1)} %param.8) | data formatting | bytes 4194304 | tf_op args[0]
  11.4 5.3 %all-to-all-start = ((bf16[128,8,1024]{0,2,1:T(8,128)(2,1)}), bf16[128,8,1024]{0,2,1:T(8,128)(2,1)}, u32[]{:S(2)}, u32[]{:S(2)}) async-start(bf16[128,8,1024]{0,2,1:T(8,128)(2,1)} %bitcast.105), calls=%async_computation | async-start | bytes 4194304 | tf_op jit(solution)/shard_map/all_to_all | solution.py:93
  16.8 29.6 %all-gather.1 = s32[8,3,8]{2,1,0:T(4,128)S(1)} all-gather(s32[1,3,8]{2,1,0:T(4,128)S(1)} %add_bitcast_fusion), channel_id=2, replica_groups=mesh['dp'=8,'fsdp'=4] {'dp'}, dimensions={0}, use_global_device_ids=true | all-gather | bytes 864 | tf_op jit(solution)/shard_map/all_gather | solution.py:92
  47.6 1.4 copy.127
  49.0 3.4 %fusion.33 = (f32[4,8,128]{2,1,0:T(8,128)S(1)}, f32[4,8,128,128]{2,3,1,0:T(8,128)}) fusion(pred[128,128]{0,1:T(8,128)(4,1)S(1)} %copy-done.4, bf16[128,4,128,1]{0,2,3,1:T(8,128)(2,1)S(1)} %copy.113, bf16[128,4,8,128]{0,3,2,1:T(8,128)(2,1)} %bitcast.111), kind=kOutput, calls=%fused_computation.63 | convolution fusion | flops 136315008 | bytes 3309568 | tf_op jit(solution)/shard_map/sub | solution.py:30
  52.4 1.6 copy.128
  54.1 2.7 %fusion.10 = bf16[4,128,128]{1,2,0:T(8,128)(2,1)} fusion(bf16[128,4,8,128]{0,3,2,1:T(8,128)(2,1)S(1)} %bitcast.106, f32[4,8,128,128]{2,3,1,0:T(8,128)} %get-tuple-element.38, f32[4,8,128]{2,1,0:T(8,128)S(1)} %get-tuple-element.37), kind=kOutput, calls=%fused_computation.21 | convolution fusion | flops 135331840 | bytes 3293184 | tf_op jit(solution)/shard_map/lbjm,jlbw->mlw/dot_general | solution.py:42
  56.9 1.4 collective-permute-start
  58.6 3.9 %copy.91 = bf16[8,128,1024]{2,1,0:T(8,128)(2,1)} copy(bf16[8,128,1024]{1,2,0:T(8,128)(2,1)} %bitcast.7) | data formatting | bytes 4194304 | tf_op jit(solution)/shard_map/all_to_all | solution.py:93
  62.5 5.3 %fusion.7 = bf16[1024,1024]{1,0:T(8,128)(2,1)} fusion(bf16[1024,1024]{1,0:T(8,128)(2,1)} %bitcast.110, s32[1024]{0:T(1024)S(1)} %bitcast.128), kind=kOutput, calls=%fused_computation.12 | convolution fusion | flops 2149580800 | bytes 4198400 | tf_op jit(solution)/shard_map/dot_general | solution.py:108
  67.8 15.0 %all-gather.4.cloned.1.call-done = bf16[1024,512]{0,1:T(8,128)(2,1)} async-done(((bf16[128,512]{0,1:T(8,128)(2,1)}), bf16[1024,512]{0,1:T(8,128)(2,1)}) %all-gather.4.cloned.1.call-update) | async-done | bytes 1048592 | tf_op jit(solution)/shard_map/all_gather | solution.py:121
  82.8 4.4 %fusion.35 = f32[1024,512]{1,0:T(8,128)} fusion(bf16[1024,1024]{1,0:T(8,128)(2,1)} %fusion.7, bf16[1024,512]{0,1:T(8,128)(2,1)} %all-gather.4.cloned.1.call-done), kind=kOutput, calls=%fused_computation.65 | convolution fusion | flops 1073741824 | bytes 5242880 | tf_op jit(solution)/shard_map/dot_general | solution.py:123
  87.3 1.6 collective-permute-start.1
  88.8 8.7 %collective-permute-done.1 = bf16[256,512]{1,0:T(8,128)(2,1)S(1)} collective-permute-done((bf16[256,512]{1,0:T(8,128)(2,1)}, bf16[256,512]{1,0:T(8,128)(2,1)S(1)}, u32[]{:S(2)}, u32[]{:S(2)}) %collective-permute-start.1) | collective-permute-done | bytes 262176 | tf_op jit(solution)/shard_map/ppermute | solution.py:101
  97.5 2.0 maximum_select_fusion.1
  99.4 3.3 %collective-permute-start.2 = (bf16[512,512]{1,0:T(8,128)(2,1)}, bf16[512,512]{1,0:T(8,128)(2,1)}, u32[]{:S(2)}, u32[]{:S(2)}) collective-permute-start(bf16[512,512]{1,0:T(8,128)(2,1)} %maximum_select_fusion.1), channel_id=1, source_target_pairs={{0,2},{1,3},{2,0},{3,1},{4,6},{5,7},{6,4},{7,5},{8,10},{9,11},{10,... | collective-permute-start | bytes 1572872 | tf_op jit(solution)/shard_map/ppermute | solution.py:101
  102.7 48.2 %collective-permute-done.2 = bf16[512,512]{1,0:T(8,128)(2,1)} collective-permute-done((bf16[512,512]{1,0:T(8,128)(2,1)}, bf16[512,512]{1,0:T(8,128)(2,1)}, u32[]{:S(2)}, u32[]{:S(2)}) %collective-permute-start.2) | collective-permute-done | bytes 524320 | tf_op jit(solution)/shard_map/ppermute | solution.py:101
  150.9 4.4 %convolution_convert_fusion.3 = bf16[1024,512]{1,0:T(8,128)(2,1)} fusion(bf16[1024,1024]{1,0:T(8,128)(2,1)} %fusion.7, bf16[512,512]{1,0:T(8,128)(2,1)} %collective-permute-done.2, bf16[512,512]{1,0:T(8,128)(2,1)} %maximum_select_fusion.1, pred[]{:T(512)S(6)} %eq.47), kind=kOutput, calls=%fused_computation.17 | convolution fusion | flops 1078984704 | bytes 4194305 | tf_op jit(solution)/shard_map/dot_general | solution.py:109
  155.3 4.2 %all-to-all-start.1 = ((bf16[8,128,512]{2,1,0:T(8,128)(2,1)}), bf16[8,128,512]{2,1,0:T(8,128)(2,1)}, u32[]{:S(2)}, u32[]{:S(2)}) async-start(bf16[8,128,512]{2,1,0:T(8,128)(2,1)} %bitcast.113), calls=%async_computation.1 | async-start | bytes 2097152 | tf_op jit(solution)/shard_map/all_to_all | solution.py:110
  159.5 4.5 %convolution_convert_fusion = bf16[1024,1024]{1,0:T(8,128)(2,1)} fusion(bf16[1024,512]{0,1:T(8,128)(2,1)} %all-gather.4.cloned.1.call-done, bf16[512,512]{1,0:T(8,128)(2,1)} %collective-permute-done.2, bf16[512,512]{1,0:T(8,128)(2,1)} %maximum_select_fusion.1, pred[]{:T(512)S(6)} %eq.47), kind=kOutput, calls=%fused_computation.13 | convolution fusion | flops 1079508992 | bytes 4194305 | tf_op jit(solution)/shard_map/dot_general | solution.py:131
  164.0 10.9 %all-to-all-done.1 = bf16[8,128,512]{2,1,0:T(8,128)(2,1)} async-done(((bf16[8,128,512]{2,1,0:T(8,128)(2,1)}), bf16[8,128,512]{2,1,0:T(8,128)(2,1)}, u32[]{:S(2)}, u32[]{:S(2)}) %all-to-all-start.1) | async-done | bytes 1048608 | tf_op jit(solution)/shard_map/all_to_all | solution.py:110
  175.0 4.7 %all-to-all-start.2 = ((bf16[8,128,1024]{2,1,0:T(8,128)(2,1)}), bf16[8,128,1024]{2,1,0:T(8,128)(2,1)}, u32[]{:S(2)}, u32[]{:S(2)}) async-start(bf16[8,128,1024]{2,1,0:T(8,128)(2,1)} %bitcast.108), calls=%async_computation.2 | async-start | bytes 4194304 | tf_op jit(solution)/shard_map/all_to_all | solution.py:134
  179.6 1.4 reduce_sum.80
  181.1 3.0 %convolution_convert_fusion.2 = bf16[4,128,8,128]{3,1,2,0:T(8,128)(2,1)} fusion(bf16[128,4,128,1]{0,2,3,1:T(8,128)(2,1)S(1)} %bitcast.116, f32[4,8,128,128]{2,3,1,0:T(8,128)} %get-tuple-element.38, f32[4,8,128]{2,1,0:T(8,128)S(1)} %copy-done.9), kind=kOutput, calls=%fused_computation.16 | convolution fusion | flops 135790592 | bytes 3293184 | tf_op jit(solution)/shard_map/yxmd,dya->myxa/dot_general | solution.py:33
  184.1 2.3 %copy.105 = bf16[128,4096]{1,0:T(8,128)(2,1)} copy(bf16[128,4096]{0,1:T(8,128)(2,1)} %bitcast.115) | data formatting | bytes 2097152
  186.4 1.8 fusion.34
  188.2 5.4 %convolution_convert_fusion.1 = bf16[4,8,128,128]{2,3,1,0:T(8,128)(2,1)} fusion(bf16[128,4,128,1]{0,2,3,1:T(8,128)(2,1)S(1)} %copy.113, f32[4,128,128,8]{2,1,3,0:T(8,128)} %fusion.34, f32[4,8,128,128]{2,3,1,0:T(8,128)} %get-tuple-element.38, f32[4,8,128]{2,1,0:T(8,128)S(1)} %copy-done.9), kind=kOutput, calls=%fused_computation.15 | convolution fusion | flops 138416256 | bytes 5390336 | tf_op jit(solution)/shard_map/yxmd,dya->myxa/dot_general | solution.py:50
  193.6 2.4 %copy.106 = bf16[128,4096]{1,0:T(8,128)(2,1)} copy(bf16[128,4096]{0,1:T(8,128)(2,1)} %bitcast.114) | data formatting | bytes 2097152
  195.9 4.3 %fusion.9 = bf16[4,128,128]{1,2,0:T(8,128)(2,1)S(1)} fusion(bf16[128,4,8,128]{0,3,2,1:T(8,128)(2,1)S(1)} %bitcast.112, f32[4,128,128,8]{2,1,3,0:T(8,128)} %fusion.34, f32[4,8,128,128]{2,3,1,0:T(8,128)} %get-tuple-element.38, f32[4,8,128]{2,1,0:T(8,128)S(1)} %copy-done.9), kind=kOutput, calls=%fused_computation.20 | convolution fusion | flops 137957504 | bytes 5390336 | tf_op jit(solution)/shard_map/lbjm,jlbw->mlw/dot_general | solution.py:53
  201.0 5.1 %all-to-all-done.2 = bf16[8,128,1024]{2,1,0:T(8,128)(2,1)} async-done(((bf16[8,128,1024]{2,1,0:T(8,128)(2,1)}), bf16[8,128,1024]{2,1,0:T(8,128)(2,1)}, u32[]{:S(2)}, u32[]{:S(2)}) %all-to-all-start.2) | async-done | bytes 2097184 | tf_op jit(solution)/shard_map/all_to_all | solution.py:134
  206.1 3.1 %copy.129 = bf16[8,16,8,1024]{3,2,0,1:T(8,128)(2,1)} copy(bf16[8,16,8,1024]{3,2,1,0:T(8,128)(2,1)} %bitcast.49) | data formatting | bytes 4194304 | tf_op jit(solution)/shard_map/all_to_all | solution.py:134
  209.3 1.9 broadcast_multiply_fusion
  (42 shorter events, 2.6 us)
Async XLA Ops:
  7.2 49.7 %copy-start = (bf16[2048,512]{1,0:T(8,128)(2,1)S(1)}, bf16[2048,512]{1,0:T(8,128)(2,1)}, u32[]{:S(2)}) copy-start(bf16[2048,512]{1,0:T(8,128)(2,1)} %param.14) | copy-start | bytes 6291460
  11.4 5.4 %copy-start.5 = (s32[1,8]{1,0:T(1,128)S(1)}, s32[1,8]{1,0:T(1,128)}, u32[]{:S(2)}) copy-start(s32[1,8]{1,0:T(1,128)} %param.11) | copy-start | bytes 100
  11.4 5.4 %copy-start.6 = (s32[1,8]{1,0:T(1,128)S(1)}, s32[1,8]{1,0:T(1,128)}, u32[]{:S(2)}) copy-start(s32[1,8]{1,0:T(1,128)} %param.10) | copy-start | bytes 100
  11.4 5.4 %copy-start.7 = (s32[1,8]{1,0:T(1,128)S(1)}, s32[1,8]{1,0:T(1,128)}, u32[]{:S(2)}) copy-start(s32[1,8]{1,0:T(1,128)} %param.9) | copy-start | bytes 100
  11.4 36.0 %copy-start.3 = (bf16[128,512]{1,0:T(8,128)(2,1)S(1)}, bf16[128,512]{1,0:T(8,128)(2,1)}, u32[]{:S(2)}) copy-start(bf16[128,512]{1,0:T(8,128)(2,1)} %param.13) | copy-start | bytes 393220
  11.4 36.2 %copy-start.1 = (bf16[128,4096]{1,0:T(8,128)(2,1)S(1)}, bf16[128,4096]{1,0:T(8,128)(2,1)}, u32[]{:S(2)}) copy-start(bf16[128,4096]{1,0:T(8,128)(2,1)} %param.12) | copy-start | bytes 3145732
  11.4 47.2 %all-to-all-start = ((bf16[128,8,1024]{0,2,1:T(8,128)(2,1)}), bf16[128,8,1024]{0,2,1:T(8,128)(2,1)}, u32[]{:S(2)}, u32[]{:S(2)}) async-start(bf16[128,8,1024]{0,2,1:T(8,128)(2,1)} %bitcast.105), calls=%async_computation | async-start | bytes 4194304 | tf_op jit(solution)/shard_map/all_to_all | solution.py:93
  16.7 66.1 %all-gather.4.cloned.1.call-start = ((), (), s32[]{:S(2)}) async-start(), calls=%async_computation.4 | async-start | bytes 1179648 | tf_op jit(solution)/shard_map/all_gather | solution.py:121
  47.5 1.6 copy-start.4
  52.4 4.3 %copy-start.8 = (f32[4,8,128]{2,1,0:T(8,128)}, f32[4,8,128]{2,1,0:T(8,128)S(1)}, u32[]{:S(2)}) copy-start(f32[4,8,128]{2,1,0:T(8,128)S(1)} %get-tuple-element.37) | copy-start | bytes 49156
  56.8 152.5 %reduce-scatter.2.cloned.1.call-start = ((), (), s32[]{:S(2)}) async-start(), calls=%async_computation.5 | async-start | bytes 2621440 | tf_op jit(solution)/shard_map/reduce_scatter | solution.py:122
  56.9 30.4 %collective-permute-start = (bf16[256,512]{1,0:T(8,128)(2,1)S(1)}, bf16[256,512]{1,0:T(8,128)(2,1)}, u32[]{:S(2)}, u32[]{:S(2)}) collective-permute-start(bf16[256,512]{1,0:T(8,128)(2,1)S(1)} %constant_dynamic-slice_fusion), channel_id=1, source_target_pairs={{0,0},{1,8},{2,16},{3,24},{4,1},{5,9},{6,17},{7,25},{8,2},{9,10},{... | collective-permute-start | bytes 786440 | tf_op jit(solution)/shard_map/ppermute | solution.py:97
  87.3 10.2 %collective-permute-start.1 = (bf16[256,512]{1,0:T(8,128)(2,1)}, bf16[256,512]{1,0:T(8,128)(2,1)S(1)}, u32[]{:S(2)}, u32[]{:S(2)}) collective-permute-start(bf16[256,512]{1,0:T(8,128)(2,1)} %collective-permute-done), channel_id=1, source_target_pairs={{0,1},{1,0},{2,3},{3,2},{4,5},{5,4},{6,7},{7,6},{8,9},{9,8},{10,11... | collective-permute-start | bytes 786440 | tf_op jit(solution)/shard_map/ppermute | solution.py:101
  99.4 51.5 %collective-permute-start.2 = (bf16[512,512]{1,0:T(8,128)(2,1)}, bf16[512,512]{1,0:T(8,128)(2,1)}, u32[]{:S(2)}, u32[]{:S(2)}) collective-permute-start(bf16[512,512]{1,0:T(8,128)(2,1)} %maximum_select_fusion.1), channel_id=1, source_target_pairs={{0,2},{1,3},{2,0},{3,1},{4,6},{5,7},{6,4},{7,5},{8,10},{9,11},{10,... | collective-permute-start | bytes 1572872 | tf_op jit(solution)/shard_map/ppermute | solution.py:101
  155.3 19.7 %all-to-all-start.1 = ((bf16[8,128,512]{2,1,0:T(8,128)(2,1)}), bf16[8,128,512]{2,1,0:T(8,128)(2,1)}, u32[]{:S(2)}, u32[]{:S(2)}) async-start(bf16[8,128,512]{2,1,0:T(8,128)(2,1)} %bitcast.113), calls=%async_computation.1 | async-start | bytes 2097152 | tf_op jit(solution)/shard_map/all_to_all | solution.py:110
  175.0 6.2 %copy-start.9 = (f32[4,8,128]{2,1,0:T(8,128)S(1)}, f32[4,8,128]{2,1,0:T(8,128)}, u32[]{:S(2)}) copy-start(f32[4,8,128]{2,1,0:T(8,128)} %copy-done.8) | copy-start | bytes 49156
  175.0 31.1 %all-to-all-start.2 = ((bf16[8,128,1024]{2,1,0:T(8,128)(2,1)}), bf16[8,128,1024]{2,1,0:T(8,128)(2,1)}, u32[]{:S(2)}, u32[]{:S(2)}) async-start(bf16[8,128,1024]{2,1,0:T(8,128)(2,1)} %bitcast.108), calls=%async_computation.2 | async-start | bytes 4194304 | tf_op jit(solution)/shard_map/all_to_all | solution.py:134
  193.6 2.4 %copy-start.2 = (bf16[128,4096]{0,1:T(8,128)(2,1)S(1)}, bf16[128,4096]{0,1:T(8,128)(2,1)}, u32[]{:S(2)}) copy-start(bf16[128,4096]{0,1:T(8,128)(2,1)} %copy.127) | copy-start | bytes 3145732
Sparse Core Ops, SparseCore 0:
  56.9 25.8 all-gather.3
  87.4 61.2 reduce-scatter.1
